TPU v7x, 32 devices: a whole 2x2x4 slice. The times are simulated.
32 devices in a mesh: lon: 8 (over z, core), lat: 4 (over y, x).
Axes of the slice: x: 2, y: 2, z: 4, core: 2. Of those that a mesh axis runs over, the one named last changes fastest.
Arguments:
- land_sea: int32 [512, 1792], P('lat', 'lon'), may hold values from 0 to 1, as said below
- obs_cell: int32 [4, 8, 2048], P('lat', 'lon'), may hold values from 0 to 28671
- obs_value: float32 [4, 8, 2048], P('lat', 'lon'), may hold values from -12 to 12
- obs_weight: float32 [4, 8, 2048], P('lat', 'lon'), may hold values from 0.5 to 4
- intersection: int32 [4, 8], P('lat', 'lon'), may hold values from 1 to 16, as said below
- factors: float32 [40, 16, 16, 2048], P('lat', None, None, 'lon'), may hold values from -1 to 1, as said below
- coarse_inverse: float32 [512, 512], P(('lon', 'lat')), may hold values from -1 to 1, as said below
Outputs:
- solution: float32 [512, 1792], P('lat', 'lon')
- residual: float32 [512, 1792], P('lat', 'lon')
- preconditioned: float32 [512, 1792], P('lat', 'lon')
Inputs may be any that keep to these rules, and one draw needn't show every extreme that they name: `land_sea`: 1 marks ocean and 0 land; the first and last rows of the grid are land. Some tile has intersection 16. `factors`: each block is lower triangular (zero where the third index exceeds the second) with a positive diagonal. `coarse_inverse`: symmetric and positive definite.
All inputs are finite; a program needn't handle non-finite values.
Results may differ from a plain program's by a relative error of at most 0.00012.
Values sent between devices are 32-bit elements; how exact they have to be, the bound alone decides.
A program may use at most 64 MiB of HBM per device.

v0:
```python
import jax
import jax.numpy as jnp
from jax import lax
from jax.sharding import PartitionSpec as P

HW = 16
SUB = 4


DAMPING = 0.02


def with_halo(x, sides, width):
    for axis, dim in sides:
        size, length = (lax.axis_size(axis), x.shape[dim])
        up = [(i, (i + 1) % size) for i in range(size)]
        down = [(j, i) for i, j in up]
        last = lax.slice_in_dim(x, length - width, length, axis=dim)
        initial = lax.slice_in_dim(x, 0, width, axis=dim)
        before = lax.ppermute(last, axis, up)
        after = lax.ppermute(initial, axis, down)
        x = jnp.concatenate([before, x, after], axis=dim)
    return x


def with_faces(field):
    return with_halo(field, (("lon", 1), ("lat", 0)), 1)


def with_margin(field):
    return with_halo(field, (("lon", 1), ("lat", 0)), HW)


def fold_rows(back):
    length = back.shape[0] - 4 * HW
    inner = back[2 * HW : 2 * HW + length]
    head = jnp.pad(back[:HW], ((0, length - HW), (0, 0)))
    tail = jnp.pad(back[length + 3 * HW :], ((length - HW, 0), (0, 0)))
    return inner + head + tail


def fold_cols(back):
    length = back.shape[1] - 4 * HW
    inner = back[:, 2 * HW : 2 * HW + length]
    head = jnp.pad(back[:, :HW], ((0, 0), (0, length - HW)))
    tail = jnp.pad(back[:, length + 3 * HW :], ((0, 0), (length - HW, 0)))
    return inner + head + tail


def body(land_sea, obs_cell, obs_value, obs_weight, intersection, factors, coarse_inverse):
    ocean_mask = land_sea.astype(jnp.float32)
    tile_rows, tile_cols = land_sea.shape
    cells = obs_cell[0, 0]
    obs_diag = jax.ops.segment_sum(
        obs_weight[0, 0], cells, num_segments=tile_rows * tile_cols
    ).reshape(tile_rows, tile_cols)
    obs_load = jax.ops.segment_sum(
        obs_weight[0, 0] * obs_value[0, 0], cells, num_segments=tile_rows * tile_cols
    ).reshape(tile_rows, tile_cols)
    rhs = ocean_mask * obs_load
    ocean_pad = with_faces(ocean_mask)
    east = ocean_mask * ocean_pad[1:-1, 2:]
    west = ocean_mask * ocean_pad[1:-1, :-2]
    north = ocean_mask * ocean_pad[:-2, 1:-1]
    south = ocean_mask * ocean_pad[2:, 1:-1]
    total_conduct = east + west + north + south
    mask_wide = with_margin(ocean_mask)
    lat_index = lax.axis_index("lat")
    lat_count = lax.axis_size("lat")
    row_pos = jnp.arange(tile_rows + 2 * HW, dtype=jnp.int32)
    col_pos = jnp.arange(tile_cols + 2 * HW, dtype=jnp.int32)
    reach = intersection[0, 0]
    global_row = lat_index * tile_rows + row_pos - HW
    row_ok = (
        (row_pos >= HW - reach)
        & (row_pos < HW + tile_rows + reach)
        & (global_row >= 0)
        & (global_row < lat_count * tile_rows)
    )
    col_ok = (col_pos >= HW - reach) & (col_pos < HW + tile_cols + reach)
    weights = mask_wide * row_ok[:, None].astype(jnp.float32) * col_ok[None, :].astype(jnp.float32)
    block_count, block_size = (factors.shape[0], factors.shape[1])
    coarse_rows = coarse_inverse.shape[0]
    residual = rhs
    wide = with_margin(residual)
    source = (weights * wide).reshape(block_count, block_size, wide.shape[1])
    forward = jnp.einsum("kabx,kbx->kax", factors, source, precision=lax.Precision.HIGHEST)
    solved = jnp.einsum("kabx,kax->kbx", factors, forward, precision=lax.Precision.HIGHEST)
    contrib = weights * solved.reshape(wide.shape)
    back = with_halo(contrib, (("lon", 1), ("lat", 0)), HW)
    local = fold_cols(fold_rows(back))
    sums = jnp.sum(
        (ocean_mask * residual).reshape(SUB, tile_rows // SUB, SUB, tile_cols // SUB), axis=(1, 3)
    ).reshape(coarse_rows)
    answer = lax.psum_scatter(
        jnp.dot(
            sums,
            coarse_inverse,
            precision=lax.Precision.HIGHEST,
            preferred_element_type=jnp.float32,
        ),
        ("lon", "lat"),
        scatter_dimension=0,
        tiled=True,
    )
    spread = jnp.broadcast_to(
        answer.reshape(SUB, 1, SUB, 1), (SUB, tile_rows // SUB, SUB, tile_cols // SUB)
    )
    precond = local + ocean_mask * spread.reshape(tile_rows, tile_cols)
    affinity = lax.psum(jnp.sum(residual * precond), ("lon", "lat"))
    padded = with_faces(precond)
    beside = (
        east * padded[1:-1, 2:]
        + west * padded[1:-1, :-2]
        + north * padded[:-2, 1:-1]
        + south * padded[2:, 1:-1]
    )
    coupling = total_conduct * precond - beside
    image = ocean_mask * ((obs_diag + DAMPING) * precond + coupling) + (1.0 - ocean_mask) * precond
    alpha = affinity / lax.psum(jnp.sum(precond * image), ("lon", "lat"))
    solution = alpha * precond
    residual = residual - alpha * image
    return (solution, residual, precond)


def solution(mesh):
    in_specs = (
        P("lat", "lon"),
        P("lat", "lon", None),
        P("lat", "lon", None),
        P("lat", "lon", None),
        P("lat", "lon"),
        P("lat", None, None, "lon"),
        P(("lon", "lat"), None),
    )
    out_specs = (P("lat", "lon"), P("lat", "lon"), P("lat", "lon"))
    return jax.shard_map(body, mesh=mesh, in_specs=in_specs, out_specs=out_specs, check_vma=False)
```

profile of v0, /device:TPU:0, one launch (start us, length us, event | category | flops | bytes accessed | tf_op | source)
XLA Modules:
  0.0 151.2 jit_solution(7972346232530367683)
XLA Ops:
  0.7 0.9 mul.100
  1.5 11.4 %scatter_custom_fusion = f32[28672]{0:T(1024)S(1)} fusion(s32[2048]{0:T(1024)} %bitcast.30, f32[2048]{0:T(1024)S(1)} %mul.100, f32[]{:T(128)} %constant.13.clone.1), kind=kCustom, calls=%fused_computation.55 | custom fusion | flops 2048 | bytes 115200 | tf_op jit(solution)/shard_map/scatter-add | solution.py:57
  13.0 1.0 copy.19
  14.0 0.7 convert_multiply_fusion
  14.7 0.7 fusion.39
  15.9 4.0 %collective-permute-start.5 = (f32[128,16]{1,0:T(8,128)}, f32[128,16]{1,0:T(8,128)}, u32[]{:S(2)}, u32[]{:S(2)}) collective-permute-start(f32[128,16]{1,0:T(8,128)} %get-tuple-element.38), channel_id=1, source_target_pairs={{4,0},{8,4},{12,8},{16,12},{20,16},{24,20},{28,24},{0,28},{5,1},{9... | collective-permute-start | bytes 24584 | tf_op jit(solution)/shard_map/ppermute | solution.py:21
  19.9 0.7 fusion.38
  20.6 3.5 %collective-permute-start.1 = (f32[128,16]{1,0:T(8,128)}, f32[128,16]{1,0:T(8,128)S(1)}, u32[]{:S(2)}, u32[]{:S(2)}) collective-permute-start(f32[128,16]{1,0:T(8,128)} %get-tuple-element.36), channel_id=1, source_target_pairs={{4,0},{8,4},{12,8},{16,12},{20,16},{24,20},{28,24},{0,28},{5,1},{9... | collective-permute-start | bytes 24584 | tf_op jit(solution)/shard_map/ppermute | solution.py:21
  24.2 0.7 fusion.36
  25.6 1.1 reshape.75
  27.5 0.8 pad_maximum_fusion.23
  28.3 2.0 %collective-permute-start.6 = (f32[16,256]{1,0:T(8,128)S(1)}, f32[16,256]{1,0:T(8,128)S(1)}, u32[]{:S(2)}, u32[]{:S(2)}) collective-permute-start(f32[16,256]{1,0:T(8,128)S(1)} %get-tuple-element.27), channel_id=1, source_target_pairs={{0,1},{1,2},{2,3},{3,0},{4,5},{5,6},{6,7},{7,4},{8,9},{9,10},{10,1... | collective-permute-start | bytes 49160 | tf_op jit(solution)/shard_map/ppermute | solution.py:20
  30.3 1.0 collective-permute-start.7
  31.4 1.0 collective-permute-start.2
  33.0 2.0 %collective-permute-start.3 = (f32[16,256]{1,0:T(8,128)S(1)}, f32[16,256]{1,0:T(8,128)S(1)}, u32[]{:S(2)}, u32[]{:S(2)}) collective-permute-start(f32[16,256]{1,0:T(8,128)S(1)} %get-tuple-element.26), channel_id=1, source_target_pairs={{1,0},{2,1},{3,2},{0,3},{5,4},{6,5},{7,6},{4,7},{9,8},{10,9},{11,1... | collective-permute-start | bytes 49160 | tf_op jit(solution)/shard_map/ppermute | solution.py:21
  35.0 1.0 pad_maximum_fusion.2
  37.0 0.7 multiply_reduce_fusion.1
  38.5 3.5 %collective-permute-start.9 = (f32[160,16]{1,0:T(8,128)S(1)}, f32[160,16]{1,0:T(8,128)S(1)}, u32[]{:S(2)}, u32[]{:S(2)}) collective-permute-start(f32[160,16]{1,0:T(8,128)S(1)} %get-tuple-element.30), channel_id=1, source_target_pairs={{4,0},{8,4},{12,8},{16,12},{20,16},{24,20},{28,24},{0,28},{5,1},{9... | collective-permute-start | bytes 30728 | tf_op jit(solution)/shard_map/ppermute | solution.py:21
  42.2 38.3 %all-reduce.3 = f32[512]{0:T(512)S(1)} all-reduce(f32[512]{0:T(512)S(1)} %bitcast.29), channel_id=2, replica_groups=mesh['lon'=8,'lat'=4] {'lon','lat'}, use_global_device_ids=true, to_apply=%region_2.3.clone | all-reduce | flops 512 | bytes 4096
  81.0 2.3 %collective-permute-start.10 = (f32[16,288]{1,0:T(8,128)S(1)}, f32[16,288]{1,0:T(8,128)S(1)}, u32[]{:S(2)}, u32[]{:S(2)}) collective-permute-start(f32[16,288]{1,0:T(8,128)S(1)} %get-tuple-element.19), channel_id=1, source_target_pairs={{0,1},{1,2},{2,3},{3,0},{4,5},{5,6},{6,7},{7,4},{8,9},{9,10},{10,1... | collective-permute-start | bytes 55304 | tf_op jit(solution)/shard_map/ppermute | solution.py:20
  83.4 0.8 collective-permute-start.11
  84.3 1.6 %collective-permute-done.10 = f32[16,288]{1,0:T(8,128)S(1)} collective-permute-done((f32[16,288]{1,0:T(8,128)S(1)}, f32[16,288]{1,0:T(8,128)S(1)}, u32[]{:S(2)}, u32[]{:S(2)}) %collective-permute-start.10) | collective-permute-done | bytes 18464 | tf_op jit(solution)/shard_map/ppermute | solution.py:20
  85.9 1.3 collective-permute-done.11
  88.1 2.4 %collective-permute-start.14 = (f32[1,226]{1,0:T(1,128)S(1)}, f32[1,226]{1,0:T(1,128)S(1)}, u32[]{:S(2)}, u32[]{:S(2)}) collective-permute-start(f32[1,226]{1,0:T(1,128)S(1)} %get-tuple-element.21), channel_id=1, source_target_pairs={{0,1},{1,2},{2,3},{3,0},{4,5},{5,6},{6,7},{7,4},{8,9},{9,10},{10,1... | collective-permute-start | bytes 2720 | tf_op jit(solution)/shard_map/ppermute | solution.py:20
  91.1 2.2 %collective-permute-done.17 = f32[128,1]{1,0:T(8,128)S(1)} collective-permute-done((f32[128,1]{1,0:T(8,128)S(1)}, f32[128,1]{1,0:T(8,128)S(1)}, u32[]{:S(2)}, u32[]{:S(2)}) %collective-permute-start.17) | collective-permute-done | bytes 544 | tf_op jit(solution)/shard_map/ppermute | solution.py:20
  93.3 2.4 %collective-permute-start.18 = (f32[1,226]{1,0:T(1,128)S(1)}, f32[1,226]{1,0:T(1,128)S(1)}, u32[]{:S(2)}, u32[]{:S(2)}) collective-permute-start(f32[1,226]{1,0:T(1,128)S(1)} %get-tuple-element.23), channel_id=1, source_target_pairs={{0,1},{1,2},{2,3},{3,0},{4,5},{5,6},{6,7},{7,4},{8,9},{9,10},{10,1... | collective-permute-start | bytes 2720 | tf_op jit(solution)/shard_map/ppermute | solution.py:20
  96.3 11.4 %scatter_custom_fusion.1 = f32[28672]{0:T(1024)S(1)} fusion(s32[2048]{0:T(1024)} %bitcast.31, f32[2048]{0:T(1024)} %bitcast.28, f32[]{:T(128)} %constant.35.clone.1), kind=kCustom, calls=%fused_computation.53 | custom fusion | flops 2048 | bytes 115200 | tf_op jit(solution)/shard_map/scatter-add | solution.py:54
  107.8 0.7 copy.22
  108.5 1.0 multiply_reduce_fusion.2
  109.5 38.8 %all-reduce.4 = (f32[]{:T(128)}, f32[]{:T(128)}) all-reduce(f32[]{:T(128)} %get-tuple-element.13, f32[]{:T(128)} %get-tuple-element.12), channel_id=1, replica_groups=mesh['lon'=8,'lat'=4] {'lon','lat'}, use_global_device_ids=true, to_apply=%region_4.5 | all-reduce | flops 2 | bytes 16 | tf_op jit(solution)/shard_map/psum | solution.py:110
  149.8 0.7 copy.20
  150.5 0.7 copy.21
  (60 shorter events, 6.8 us)
Async XLA Ops:
  0.6 41.4 %copy-start = (f32[16,512]{1,0:T(8,128)S(1)}, f32[16,512]{1,0:T(8,128)}, u32[]{:S(2)}) copy-start(f32[16,512]{1,0:T(8,128)} %param.13) | copy-start | bytes 98308
  0.6 36.4 %copy-start.1 = (f32[10,16,16,256]{3,2,1,0:T(8,128)S(1)}, f32[10,16,16,256]{3,2,1,0:T(8,128)}, u32[]{:S(2)}) copy-start(f32[10,16,16,256]{3,2,1,0:T(8,128)} %param.12) | copy-start | bytes 7864324
  15.4 11.5 %collective-permute-start.4 = (f32[128,16]{1,0:T(8,128)}, f32[128,16]{1,0:T(8,128)}, u32[]{:S(2)}, u32[]{:S(2)}) collective-permute-start(f32[128,16]{1,0:T(8,128)} %get-tuple-element.37), channel_id=1, source_target_pairs={{0,4},{4,8},{8,12},{12,16},{16,20},{20,24},{24,28},{28,0},{1,5},{5... | collective-permute-start | bytes 24584 | tf_op jit(solution)/shard_map/ppermute | solution.py:20
  15.9 11.6 %collective-permute-start.5 = (f32[128,16]{1,0:T(8,128)}, f32[128,16]{1,0:T(8,128)}, u32[]{:S(2)}, u32[]{:S(2)}) collective-permute-start(f32[128,16]{1,0:T(8,128)} %get-tuple-element.38), channel_id=1, source_target_pairs={{4,0},{8,4},{12,8},{16,12},{20,16},{24,20},{28,24},{0,28},{5,1},{9... | collective-permute-start | bytes 24584 | tf_op jit(solution)/shard_map/ppermute | solution.py:21
  20.6 9.7 %collective-permute-start = (f32[128,16]{1,0:T(8,128)}, f32[128,16]{1,0:T(8,128)S(1)}, u32[]{:S(2)}, u32[]{:S(2)}) collective-permute-start(f32[128,16]{1,0:T(8,128)} %get-tuple-element.35), channel_id=1, source_target_pairs={{0,4},{4,8},{8,12},{12,16},{16,20},{20,24},{24,28},{28,0},{1,5},{5... | collective-permute-start | bytes 24584 | tf_op jit(solution)/shard_map/ppermute | solution.py:20
  20.6 10.7 %collective-permute-start.1 = (f32[128,16]{1,0:T(8,128)}, f32[128,16]{1,0:T(8,128)S(1)}, u32[]{:S(2)}, u32[]{:S(2)}) collective-permute-start(f32[128,16]{1,0:T(8,128)} %get-tuple-element.36), channel_id=1, source_target_pairs={{4,0},{8,4},{12,8},{16,12},{20,16},{24,20},{28,24},{0,28},{5,1},{9... | collective-permute-start | bytes 24584 | tf_op jit(solution)/shard_map/ppermute | solution.py:21
  24.9 63.1 %collective-permute-start.12 = (f32[128,1]{1,0:T(8,128)}, f32[128,1]{1,0:T(8,128)S(1)}, u32[]{:S(2)}, u32[]{:S(2)}) collective-permute-start(f32[128,1]{1,0:T(8,128)} %get-tuple-element.32), channel_id=1, source_target_pairs={{4,0},{8,4},{12,8},{16,12},{20,16},{24,20},{28,24},{0,28},{5,1},{9... | collective-permute-start | bytes 1544 | tf_op jit(solution)/shard_map/ppermute | solution.py:21
  26.9 61.1 %collective-permute-start.13 = (f32[128,1]{1,0:T(8,128)}, f32[128,1]{1,0:T(8,128)S(1)}, u32[]{:S(2)}, u32[]{:S(2)}) collective-permute-start(f32[128,1]{1,0:T(8,128)} %get-tuple-element.31), channel_id=1, source_target_pairs={{0,4},{4,8},{8,12},{12,16},{16,20},{20,24},{24,28},{28,0},{1,5},{5... | collective-permute-start | bytes 1544 | tf_op jit(solution)/shard_map/ppermute | solution.py:20
  28.3 4.7 %collective-permute-start.6 = (f32[16,256]{1,0:T(8,128)S(1)}, f32[16,256]{1,0:T(8,128)S(1)}, u32[]{:S(2)}, u32[]{:S(2)}) collective-permute-start(f32[16,256]{1,0:T(8,128)S(1)} %get-tuple-element.27), channel_id=1, source_target_pairs={{0,1},{1,2},{2,3},{3,0},{4,5},{5,6},{6,7},{7,4},{8,9},{9,10},{10,1... | collective-permute-start | bytes 49160 | tf_op jit(solution)/shard_map/ppermute | solution.py:20
  30.3 4.7 %collective-permute-start.7 = (f32[16,256]{1,0:T(8,128)S(1)}, f32[16,256]{1,0:T(8,128)S(1)}, u32[]{:S(2)}, u32[]{:S(2)}) collective-permute-start(f32[16,256]{1,0:T(8,128)S(1)} %get-tuple-element.28), channel_id=1, source_target_pairs={{1,0},{2,1},{3,2},{0,3},{5,4},{6,5},{7,6},{4,7},{9,8},{10,9},{11,1... | collective-permute-start | bytes 49160 | tf_op jit(solution)/shard_map/ppermute | solution.py:21
  31.4 4.7 %collective-permute-start.2 = (f32[16,256]{1,0:T(8,128)S(1)}, f32[16,256]{1,0:T(8,128)S(1)}, u32[]{:S(2)}, u32[]{:S(2)}) collective-permute-start(f32[16,256]{1,0:T(8,128)S(1)} %get-tuple-element.25), channel_id=1, source_target_pairs={{0,1},{1,2},{2,3},{3,0},{4,5},{5,6},{6,7},{7,4},{8,9},{9,10},{10,1... | collective-permute-start | bytes 49160 | tf_op jit(solution)/shard_map/ppermute | solution.py:20
  33.0 3.8 %collective-permute-start.3 = (f32[16,256]{1,0:T(8,128)S(1)}, f32[16,256]{1,0:T(8,128)S(1)}, u32[]{:S(2)}, u32[]{:S(2)}) collective-permute-start(f32[16,256]{1,0:T(8,128)S(1)} %get-tuple-element.26), channel_id=1, source_target_pairs={{1,0},{2,1},{3,2},{0,3},{5,4},{6,5},{7,6},{4,7},{9,8},{10,9},{11,1... | collective-permute-start | bytes 49160 | tf_op jit(solution)/shard_map/ppermute | solution.py:21
  37.7 49.6 %copy-start.2 = (pred[224]{0:T(512)(128)(4,1)S(1)}, pred[224]{0:T(512)(128)(4,1)}, u32[]{:S(2)}) copy-start(pred[224]{0:T(512)(128)(4,1)} %constant.34.clone.1) | copy-start | bytes 676
  38.5 42.5 %collective-permute-start.8 = (f32[160,16]{1,0:T(8,128)S(1)}, f32[160,16]{1,0:T(8,128)S(1)}, u32[]{:S(2)}, u32[]{:S(2)}) collective-permute-start(f32[160,16]{1,0:T(8,128)S(1)} %get-tuple-element.29), channel_id=1, source_target_pairs={{0,4},{4,8},{8,12},{12,16},{16,20},{20,24},{24,28},{28,0},{1,5},{5... | collective-permute-start | bytes 30728 | tf_op jit(solution)/shard_map/ppermute | solution.py:20
  38.5 42.4 %collective-permute-start.9 = (f32[160,16]{1,0:T(8,128)S(1)}, f32[160,16]{1,0:T(8,128)S(1)}, u32[]{:S(2)}, u32[]{:S(2)}) collective-permute-start(f32[160,16]{1,0:T(8,128)S(1)} %get-tuple-element.30), channel_id=1, source_target_pairs={{4,0},{8,4},{12,8},{16,12},{20,16},{24,20},{28,24},{0,28},{5,1},{9... | collective-permute-start | bytes 30728 | tf_op jit(solution)/shard_map/ppermute | solution.py:21
  81.0 4.9 %collective-permute-start.10 = (f32[16,288]{1,0:T(8,128)S(1)}, f32[16,288]{1,0:T(8,128)S(1)}, u32[]{:S(2)}, u32[]{:S(2)}) collective-permute-start(f32[16,288]{1,0:T(8,128)S(1)} %get-tuple-element.19), channel_id=1, source_target_pairs={{0,1},{1,2},{2,3},{3,0},{4,5},{5,6},{6,7},{7,4},{8,9},{9,10},{10,1... | collective-permute-start | bytes 55304 | tf_op jit(solution)/shard_map/ppermute | solution.py:20
  83.4 3.8 %collective-permute-start.11 = (f32[16,288]{1,0:T(8,128)S(1)}, f32[16,288]{1,0:T(8,128)S(1)}, u32[]{:S(2)}, u32[]{:S(2)}) collective-permute-start(f32[16,288]{1,0:T(8,128)S(1)} %get-tuple-element.20), channel_id=1, source_target_pairs={{1,0},{2,1},{3,2},{0,3},{5,4},{6,5},{7,6},{4,7},{9,8},{10,9},{11,1... | collective-permute-start | bytes 55304 | tf_op jit(solution)/shard_map/ppermute | solution.py:21
  87.5 3.6 %collective-permute-start.16 = (f32[128,1]{1,0:T(8,128)S(1)}, f32[128,1]{1,0:T(8,128)S(1)}, u32[]{:S(2)}, u32[]{:S(2)}) collective-permute-start(f32[128,1]{1,0:T(8,128)S(1)} %get-tuple-element.34), channel_id=1, source_target_pairs={{4,0},{8,4},{12,8},{16,12},{20,16},{24,20},{28,24},{0,28},{5,1},{9... | collective-permute-start | bytes 1544 | tf_op jit(solution)/shard_map/ppermute | solution.py:21
  87.5 5.7 %collective-permute-start.17 = (f32[128,1]{1,0:T(8,128)S(1)}, f32[128,1]{1,0:T(8,128)S(1)}, u32[]{:S(2)}, u32[]{:S(2)}) collective-permute-start(f32[128,1]{1,0:T(8,128)S(1)} %get-tuple-element.33), channel_id=1, source_target_pairs={{0,4},{4,8},{8,12},{12,16},{16,20},{20,24},{24,28},{28,0},{1,5},{5... | collective-permute-start | bytes 1544 | tf_op jit(solution)/shard_map/ppermute | solution.py:20
  88.1 20.4 %collective-permute-start.14 = (f32[1,226]{1,0:T(1,128)S(1)}, f32[1,226]{1,0:T(1,128)S(1)}, u32[]{:S(2)}, u32[]{:S(2)}) collective-permute-start(f32[1,226]{1,0:T(1,128)S(1)} %get-tuple-element.21), channel_id=1, source_target_pairs={{0,1},{1,2},{2,3},{3,0},{4,5},{5,6},{6,7},{7,4},{8,9},{9,10},{10,1... | collective-permute-start | bytes 2720 | tf_op jit(solution)/shard_map/ppermute | solution.py:20
  90.5 18.0 %collective-permute-start.15 = (f32[1,226]{1,0:T(1,128)S(1)}, f32[1,226]{1,0:T(1,128)S(1)}, u32[]{:S(2)}, u32[]{:S(2)}) collective-permute-start(f32[1,226]{1,0:T(1,128)S(1)} %get-tuple-element.22), channel_id=1, source_target_pairs={{1,0},{2,1},{3,2},{0,3},{5,4},{6,5},{7,6},{4,7},{9,8},{10,9},{11,1... | collective-permute-start | bytes 2720 | tf_op jit(solution)/shard_map/ppermute | solution.py:21
  93.3 15.2 %collective-permute-start.18 = (f32[1,226]{1,0:T(1,128)S(1)}, f32[1,226]{1,0:T(1,128)S(1)}, u32[]{:S(2)}, u32[]{:S(2)}) collective-permute-start(f32[1,226]{1,0:T(1,128)S(1)} %get-tuple-element.23), channel_id=1, source_target_pairs={{0,1},{1,2},{2,3},{3,0},{4,5},{5,6},{6,7},{7,4},{8,9},{9,10},{10,1... | collective-permute-start | bytes 2720 | tf_op jit(solution)/shard_map/ppermute | solution.py:20
  95.7 12.8 %collective-permute-start.19 = (f32[1,226]{1,0:T(1,128)S(1)}, f32[1,226]{1,0:T(1,128)S(1)}, u32[]{:S(2)}, u32[]{:S(2)}) collective-permute-start(f32[1,226]{1,0:T(1,128)S(1)} %get-tuple-element.24), channel_id=1, source_target_pairs={{1,0},{2,1},{3,2},{0,3},{5,4},{6,5},{7,6},{4,7},{9,8},{10,9},{11,1... | collective-permute-start | bytes 2720 | tf_op jit(solution)/shard_map/ppermute | solution.py:21
where the time goes:
time: 152 us; the launch traced here: 151 us
  blocking collectives  77.1 us (51%)
  other arithmetic  29.5 us (19%)
  starting transfers between devices  27.8 us (18%)
  local copies, waits for them, and re-layouts  7.43 us (5%)
  waiting for transfers between devices  6.34 us (4%)
  between operations  2.9 us (2%)
    psum x1, blocking collectives, body(): affinity = lax.psum(jnp.sum(residual * precond), ('lon', 'lat'))  38.8 us
    unnamed x1, blocking collectives  38.3 us
    ppermute x10, starting transfers between devices, with_halo(): after = lax.ppermute(initial, axis, down)  16.1 us
    ppermute x10, starting transfers between devices, with_halo(): before = lax.ppermute(last, axis, up)  11.7 us
    scatter-add x1, other arithmetic, body(): jax.ops.segment_sum(obs_weight[0, 0], cells, num_segments=tile_rows * til...  11.4 us
    scatter-add x1, other arithmetic, body(): jax.ops.segment_sum(obs_weight[0, 0] * obs_value[0, 0], cells, num_segmen...  11.4 us
    ppermute x10, waiting for transfers between devices, with_halo(): before = lax.ppermute(last, axis, up)  4.41 us
    unnamed x11, local copies, waits for them, and re-layouts  3.33 us
  transfers between devices with their start and end apart: 20, of which 6 were waited for; matrix products, arithmetic and copies ran while one was open for 13% of the time, Pallas kernels for 0%

commit v1 on v0

v1 whole, which is shorter than its diff:
```python
import functools

import jax
import jax.numpy as jnp
from jax import lax
from jax.experimental import pallas as pl
from jax.experimental.pallas import tpu as pltpu
from jax.sharding import PartitionSpec as P

HW = 16
SUB = 4
DAMPING = 0.02
LANES = 128
F32 = jnp.float32
BF16 = jnp.bfloat16


def iota(shape, dim):
    return lax.broadcasted_iota(jnp.int32, shape, dim)


def kernel(
    n_lat, n_lon,
    sea_ref, cell_ref, value_ref, weight_ref, reach_ref, factors_ref, coarse_ref,
    sol_ref, res_ref, pre_ref,
    fac, diag, core, wide, edge, edge_in, rows_in, corner_in, gather,
    contrib, side_in, band_in, cross_in, total, mine, lat_in, half, lon_in,
    fac_sem, send_sem, recv_sem,
):
    cy, cx = sea_ref.shape
    h, w = cy + 2 * HW, cx + 2 * HW
    i, j = lax.axis_index("lat"), lax.axis_index("lon")

    def lat_peer(o):
        return lax.rem(i + o + n_lat, n_lat)

    def lon_peer(o):
        return lax.rem(j + o + n_lon, n_lon)

    load = pltpu.make_async_copy(factors_ref, fac, fac_sem)
    load.start()

    barrier = pltpu.get_barrier_semaphore()

    def greet(pi, pj):
        pl.semaphore_signal(
            barrier, inc=1, device_id={"lat": pi, "lon": pj}, device_id_type=pl.DeviceIdType.MESH
        )

    corners = [(-1, -1), (-1, 1), (1, -1), (1, 1)]
    for o in range(1, n_lat):
        greet(lat_peer(o), j)
    for o in range(1, n_lon):
        greet(i, lon_peer(o))
    for di, dj in corners:
        greet(lat_peer(di), lon_peer(dj))

    used = [0]

    def remote(src, dst, pi, pj):
        k = used[0]
        used[0] += 1
        copy = pltpu.make_async_remote_copy(
            src_ref=src,
            dst_ref=dst,
            send_sem=send_sem.at[k],
            recv_sem=recv_sem.at[k],
            device_id={"lat": pi, "lon": pj},
            device_id_type=pl.DeviceIdType.MESH,
        )
        copy.start()
        return copy

    core[0, :, 0:cx] = sea_ref[...].astype(F32)
    core[0, :, cx:w] = jnp.zeros((cy, w - cx), F32)
    ocean = pltpu.roll(core[0], HW, 1)
    count = cell_ref.shape[1]
    chunk = 512 if count % 512 == 0 else count
    sums = jnp.zeros((4 * cy, w), F32)
    for at in range(0, count, chunk):
        cell = cell_ref[:, at : at + chunk].astype(F32)
        row = jnp.floor((cell + 0.5) * (1.0 / cx))
        col = cell - row * cx + HW
        weight = weight_ref[:, at : at + chunk]
        product = weight * value_ref[:, at : at + chunk]
        in_row = iota((cy, chunk), 0).astype(F32) == row
        in_col = iota((w, chunk), 0).astype(F32) == col
        parts = []
        for x in (weight, product):
            high = x.astype(BF16).astype(F32)
            parts += [high, x - high]
        left = jnp.concatenate([jnp.where(in_row, x, 0.0).astype(BF16) for x in parts], axis=0)
        right = jnp.where(in_col, 1.0, 0.0).astype(BF16)
        sums = sums + lax.dot_general(
            left, right, (((1,), (1,)), ((), ())), preferred_element_type=F32
        )
    diag[...] = sums[0:cy] + sums[cy : 2 * cy]
    rhs = ocean * (sums[2 * cy : 3 * cy] + sums[3 * cy : 4 * cy])
    core[0] = ocean
    core[1] = rhs

    block = cy // SUB
    lane_w = iota((SUB, w), 1) - HW
    sub_w = iota((SUB, w), 0) * (cx // SUB)
    group = jnp.where((lane_w >= sub_w) & (lane_w < sub_w + cx // SUB), 1.0, 0.0)
    strips = [
        jnp.sum(rhs[s * block : (s + 1) * block], axis=0, keepdims=True) * group for s in range(SUB)
    ]
    own = jnp.sum(jnp.concatenate(strips, axis=0), axis=1, keepdims=True)
    entries = SUB * SUB
    spot = iota((entries, LANES), 0) == (iota((entries, LANES), 1) % entries)
    own = jnp.sum(jnp.where(spot, own, 0.0), axis=0, keepdims=True)
    gather[j, i] = jnp.broadcast_to(own, (8, LANES))

    lane = iota((cy, LANES), 1)
    hi = w - LANES
    edge[0] = jnp.where(
        lane >= LANES - HW,
        pltpu.roll(ocean[:, :LANES], LANES - 2 * HW, 1),
        pltpu.roll(rhs[:, :LANES], LANES - 3 * HW, 1),
    )
    edge[1] = jnp.where(
        lane < HW, pltpu.roll(ocean[:, hi:], 2 * HW, 1), pltpu.roll(rhs[:, hi:], 3 * HW, 1)
    )

    pl.semaphore_wait(barrier, n_lat - 1 + n_lon - 1 + 4)

    first = [remote(gather.at[j, i], gather.at[j, i], lat_peer(o), j) for o in range(1, n_lat)]
    halo = [
        remote(edge.at[0], edge_in.at[1], i, lon_peer(-1)),
        remote(edge.at[1], edge_in.at[0], i, lon_peer(1)),
        remote(core.at[:, pl.ds(0, HW)], rows_in.at[1], lat_peer(-1), j),
        remote(core.at[:, pl.ds(cy - HW, HW)], rows_in.at[0], lat_peer(1), j),
    ]
    for k, (di, dj) in enumerate(corners):
        top = 0 if di < 0 else cy - HW
        halo.append(
            remote(
                edge.at[0 if dj < 0 else 1, pl.ds(top, HW)],
                corner_in.at[3 - k],
                lat_peer(di),
                lon_peer(dj),
            )
        )
    for copy in first:
        copy.wait_recv()
    for copy in first:
        copy.wait_send()
    second = [remote(gather.at[j], gather.at[j], i, lon_peer(o)) for o in range(1, n_lon)]
    for copy in halo:
        copy.wait()

    def west(x):
        at = iota(x.shape, 1)
        return (
            jnp.where(at < HW, x, 0.0),
            jnp.where(at < HW, pltpu.roll(x, LANES - HW, 1), 0.0),
        )

    def east(x):
        at = iota(x.shape, 1)
        return (
            jnp.where(at >= LANES - HW, x, 0.0),
            jnp.where(at >= LANES - HW, pltpu.roll(x, HW, 1), 0.0),
        )

    spans = (
        (0, HW, rows_in.at[0], corner_in[0], corner_in[1], jnp.where(i > 0, 1.0, 0.0)),
        (HW, cy, core, edge_in[0], edge_in[1], None),
        (HW + cy, HW, rows_in.at[1], corner_in[2], corner_in[3], jnp.where(i < n_lat - 1, 1.0, 0.0)),
    )
    for at, size, middle, left, right, inside in spans:
        for f, (lo, up) in enumerate(zip(west(left), east(right))):
            whole = middle[f]
            if inside is not None:
                whole, lo, up = whole * inside, lo * inside, up * inside
            wide[f, at : at + size, :] = whole
            wide[f, at : at + size, 0:LANES] += lo
            wide[f, at : at + size, hi:w] += up

    reach = reach_ref[0, 0]
    load.wait()
    col_pos = iota((HW, w), 1)
    col_ok = (col_pos >= HW - reach) & (col_pos < HW + cx + reach)
    blocks, size = fac.shape[0], fac.shape[1]
    for k in range(blocks):
        at = k * size
        row_pos = iota((size, w), 0) + at
        ok = col_ok & (row_pos >= HW - reach) & (row_pos < HW + cy + reach)
        scale = jnp.where(ok, wide[0, at : at + size], 0.0)
        u = scale * wide[1, at : at + size]
        g = jnp.zeros((size, w), F32)
        for p in range(size):
            row = fac[k, p]
            g = g + row * jnp.sum(row * u, axis=0, keepdims=True)
        contrib[at : at + size, :] = scale * g

    for copy in second:
        copy.wait()
    tiles = n_lat * n_lon
    per = LANES // entries
    ring = [
        jnp.where(iota((8, LANES), 1) // entries == r, 1.0, 0.0) for r in range(per)
    ]
    answer = jnp.zeros((entries, LANES), F32)
    for k in range(tiles // per):
        piece = jnp.zeros((8, LANES), F32)
        for r in range(per):
            d = k * per + r
            piece = piece + gather[d // n_lat, d % n_lat] * ring[r]
        answer = answer + coarse_ref[:, k * LANES : (k + 1) * LANES] * jnp.concatenate(
            [piece] * (entries // 8), axis=0
        )
    answer = jnp.sum(answer, axis=1, keepdims=True)
    for s in range(SUB):
        line = jnp.sum(answer[s * SUB : (s + 1) * SUB] * group, axis=0, keepdims=True)
        at = HW + s * block
        contrib[at : at + block, :] += core[0, s * block : (s + 1) * block, :] * line

    deep = 2 * HW
    back = [
        remote(contrib.at[:, pl.ds(0, LANES)], side_in.at[1], i, lon_peer(-1)),
        remote(contrib.at[:, pl.ds(hi, LANES)], side_in.at[0], i, lon_peer(1)),
        remote(contrib.at[pl.ds(0, deep)], band_in.at[1], lat_peer(-1), j),
        remote(contrib.at[pl.ds(h - deep, deep)], band_in.at[0], lat_peer(1), j),
    ]
    for k, (di, dj) in enumerate(corners):
        top = 0 if di < 0 else h - deep
        begin = 0 if dj < 0 else hi
        back.append(
            remote(
                contrib.at[pl.ds(top, deep), pl.ds(begin, LANES)],
                cross_in.at[3 - k],
                lat_peer(di),
                lon_peer(dj),
            )
        )
    total[...] = contrib[...]
    for copy in back:
        copy.wait()

    def from_west(x):
        return jnp.where(iota(x.shape, 1) < deep, pltpu.roll(x, deep, 1), 0.0)

    def from_east(x):
        return jnp.where(iota(x.shape, 1) >= LANES - deep, pltpu.roll(x, LANES - deep, 1), 0.0)

    total[:, 0:LANES] += from_west(side_in[0])
    total[:, hi:w] += from_east(side_in[1])
    for v in range(2):
        at = v * (h - deep)
        total[at : at + deep, :] += band_in[v]
        total[at : at + deep, 0:LANES] += from_west(cross_in[2 * v])
        total[at : at + deep, hi:w] += from_east(cross_in[2 * v + 1])

    p = total[HW : HW + cy, :]
    o = core[0]
    on, os = wide[0, HW - 1 : HW - 1 + cy, :], wide[0, HW + 1 : HW + 1 + cy, :]
    mid = wide[0, HW : HW + cy, :]
    oe, ow = pltpu.roll(mid, w - 1, 1), pltpu.roll(mid, 1, 1)
    beside = (
        oe * pltpu.roll(p, w - 1, 1)
        + ow * pltpu.roll(p, 1, 1)
        + on * total[HW - 1 : HW - 1 + cy, :]
        + os * total[HW + 1 : HW + 1 + cy, :]
    )
    image = o * ((diag[...] + DAMPING) * p + ((oe + ow + on + os) * p - beside)) + (1.0 - o) * p
    at = iota((cy, w), 1)
    inner = (at >= HW) & (at < HW + cx)

    def fold(x):
        x = jnp.sum(x.reshape(cy // 8, 8, w), axis=0)
        return sum(x[:, b : b + LANES] for b in range(0, w, LANES))

    mine[0] = fold(core[1] * p)
    mine[1] = fold(jnp.where(inner, p * image, 0.0))
    third = [remote(mine, lat_in.at[o - 1], lat_peer(o), j) for o in range(1, n_lat)]
    pre_ref[...] = pltpu.roll(p, w - HW, 1)[:, 0:cx]
    partial = mine[...]
    for o in range(1, n_lat):
        third[o - 1].wait()
        partial = partial + lat_in[o - 1]
    half[...] = partial
    fourth = [remote(half, lon_in.at[o - 1], i, lon_peer(o)) for o in range(1, n_lon)]
    rhs_out = pltpu.roll(core[1], w - HW, 1)[:, 0:cx]
    image_out = pltpu.roll(image, w - HW, 1)[:, 0:cx]
    for o in range(1, n_lon):
        fourth[o - 1].wait()
        partial = partial + lon_in[o - 1]
    rho = jnp.sum(partial[0], axis=(0, 1), keepdims=True)
    curve = jnp.sum(partial[1], axis=(0, 1), keepdims=True)
    alpha = rho / curve
    sol_ref[...] = alpha * pre_ref[...]
    res_ref[...] = rhs_out - alpha * image_out


def body(land_sea, obs_cell, obs_value, obs_weight, intersection, factors, coarse_inverse):
    n_lat, n_lon = lax.axis_size("lat"), lax.axis_size("lon")
    cy, cx = land_sea.shape
    h, w = cy + 2 * HW, cx + 2 * HW
    count = obs_cell.shape[-1]
    copies = 2 * (n_lat - 1 + n_lon - 1) + 16
    vmem = pl.BlockSpec(memory_space=pltpu.VMEM)
    out = jax.ShapeDtypeStruct((cy, cx), F32)
    return pl.pallas_call(
        functools.partial(kernel, n_lat, n_lon),
        out_shape=(out, out, out),
        in_specs=[
            vmem, vmem, vmem, vmem,
            pl.BlockSpec(memory_space=pltpu.SMEM),
            pl.BlockSpec(memory_space=pl.ANY),
            vmem,
        ],
        out_specs=(vmem, vmem, vmem),
        scratch_shapes=[
            pltpu.VMEM(factors.shape, F32),
            pltpu.VMEM((cy, w), F32),
            pltpu.VMEM((2, cy, w), F32),
            pltpu.VMEM((2, h, w), F32),
            pltpu.VMEM((2, cy, LANES), F32),
            pltpu.VMEM((2, cy, LANES), F32),
            pltpu.VMEM((2, 2, HW, w), F32),
            pltpu.VMEM((4, HW, LANES), F32),
            pltpu.VMEM((n_lon, n_lat, 8, LANES), F32),
            pltpu.VMEM((h, w), F32),
            pltpu.VMEM((2, h, LANES), F32),
            pltpu.VMEM((2, 2 * HW, w), F32),
            pltpu.VMEM((4, 2 * HW, LANES), F32),
            pltpu.VMEM((h, w), F32),
            pltpu.VMEM((2, 8, LANES), F32),
            pltpu.VMEM((n_lat - 1, 2, 8, LANES), F32),
            pltpu.VMEM((2, 8, LANES), F32),
            pltpu.VMEM((n_lon - 1, 2, 8, LANES), F32),
            pltpu.SemaphoreType.DMA,
            pltpu.SemaphoreType.DMA((copies,)),
            pltpu.SemaphoreType.DMA((copies,)),
        ],
        compiler_params=pltpu.CompilerParams(
            collective_id=0, has_side_effects=True, vmem_limit_bytes=40 * 1024 * 1024
        ),
    )(
        land_sea,
        obs_cell.reshape(1, count),
        obs_value.reshape(1, count),
        obs_weight.reshape(1, count),
        intersection,
        factors,
        coarse_inverse,
    )


def solution(mesh):
    in_specs = (
        P("lat", "lon"),
        P("lat", "lon", None),
        P("lat", "lon", None),
        P("lat", "lon", None),
        P("lat", "lon"),
        P("lat", None, None, "lon"),
        P(("lon", "lat"), None),
    )
    out_specs = (P("lat", "lon"), P("lat", "lon"), P("lat", "lon"))
    return jax.shard_map(body, mesh=mesh, in_specs=in_specs, out_specs=out_specs, check_vma=False)
```

time: 152 us -> 35.2 us (0.23)
  blocking collectives: 77.1 us -> 0 us
  other arithmetic: 29.5 us -> 0 us
  starting transfers between devices: 27.8 us -> 0 us
  Pallas kernels: 0 us -> 25.7 us
  waiting for transfers between devices: 6.34 us -> 0 us
  between operations: 2.9 us -> 1.31 us
    psum x1 -> x0, blocking collectives: 38.8 us -> none  [body(): affinity = lax.psum(jnp.sum(residual * precond), ('lon', 'lat'))]
    unnamed x1 -> x0, blocking collectives: 38.3 us -> none
    ppermute x20 -> x0, starting transfers between devices: 27.8 us -> none  [the longest x10 16.1 us: with_halo(): after = lax.ppermute(initial, axis, down)]
    pallas_call x0 -> x1, Pallas kernels: none -> 25.7 us  [body(): pl.pallas_call(functools.partial(kernel, n_lat, n_lon), out_shape=(out, o...]
    scatter-add x2 -> x0, other arithmetic: 22.8 us -> none  [the longest x1 11.4 us: body(): jax.ops.segment_sum(obs_weight[0, 0], cells, num_segments=tile_rows * til...]
    ppermute x20 -> x0, waiting for transfers between devices: 6.34 us -> none  [the longest x10 4.41 us: with_halo(): before = lax.ppermute(last, axis, up)]
    slice x6 -> x0, local copies, waits for them, and re-layouts: 2.39 us -> none  [the longest x5 2.31 us: with_halo(): last = lax.slice_in_dim(x, length - width, length, axis=dim)]
    unnamed x11, local copies, waits for them, and re-layouts: 3.33 us -> 5.57 us
  transfers between devices with their start and end apart: 20 -> 0, of which waited for: 6 -> 0; matrix products, arithmetic and copies ran while one was open for 13% -> 0% of each run, Pallas kernels for 0% -> 0%
where the time goes in v1:
time: 35.2 us; the launch traced here: 34.8 us
  Pallas kernels  25.7 us (73%)
  local copies, waits for them, and re-layouts  7.81 us (22%)
  between operations  1.31 us (4%)
    pallas_call x1, Pallas kernels, body(): pl.pallas_call(functools.partial(kernel, n_lat, n_lon), out_shape=(out, o...  25.7 us
    unnamed x11, local copies, waits for them, and re-layouts  5.57 us
    pallas_call x3, local copies, waits for them, and re-layouts, body(): pl.pallas_call(functools.partial(kernel, n_lat, n_lon), out_shape=(out, o...  2.24 us

profile of v1, /device:TPU:0, one launch (start us, length us, event | category | flops | bytes accessed | tf_op | source)
XLA Modules:
  0.0 34.8 jit_solution(7597962352094898922)
XLA Ops:
  1.3 1.0 %copy.10.sea_ref = s32[128,224]{1,0:T(8,128)S(1)} copy(s32[128,224]{0,1:T(8,128)} %param.7) | data formatting | bytes 229376 | tf_op args[0]
  2.3 0.0 copy-start
  2.3 1.7 %copy-done = f32[10,16,16,256]{3,2,1,0:T(8,128)S(1)} copy-done((f32[10,16,16,256]{3,2,1,0:T(8,128)S(1)}, f32[10,16,16,256]{3,2,1,0:T(8,128)}, u32[]{:S(2)}) %copy-start) | copy-done | bytes 2621464
  4.0 0.0 copy-start.1
  4.0 0.8 %copy-done.1 = f32[16,512]{1,0:T(8,128)S(1)} copy-done((f32[16,512]{1,0:T(8,128)S(1)}, f32[16,512]{1,0:T(8,128)}, u32[]{:S(2)}) %copy-start.1) | copy-done | bytes 32792
  4.8 0.0 copy-start.2
  4.8 0.7 %copy-done.2 = s32[1,1,2048]{2,1,0:T(1,128)S(1)} copy-done((s32[1,1,2048]{2,1,0:T(1,128)S(1)}, s32[1,1,2048]{2,1,0:T(1,128)}, u32[]{:S(2)}) %copy-start.2) | copy-done | bytes 8216
  5.5 0.0 copy-start.3
  5.5 0.7 %copy-done.3 = f32[1,1,2048]{2,1,0:T(1,128)S(1)} copy-done((f32[1,1,2048]{2,1,0:T(1,128)S(1)}, f32[1,1,2048]{2,1,0:T(1,128)}, u32[]{:S(2)}) %copy-start.3) | copy-done | bytes 8216
  6.2 0.0 copy-start.4
  6.2 0.7 %copy-done.4 = f32[1,1,2048]{2,1,0:T(1,128)S(1)} copy-done((f32[1,1,2048]{2,1,0:T(1,128)S(1)}, f32[1,1,2048]{2,1,0:T(1,128)}, u32[]{:S(2)}) %copy-start.4) | copy-done | bytes 8216
  6.9 25.7 %shard_map.94 = (f32[128,224]{1,0:T(8,128)S(1)}, f32[128,224]{1,0:T(8,128)S(1)}, f32[128,224]{1,0:T(8,128)S(1)}) custom-call(s32[128,224]{1,0:T(8,128)S(1)} %copy.10.sea_ref, s32[1,2048]{1,0:T(1,128)S(1)} %bitcast.3, f32[1,2048]{1,0:T(1,128)S(1)} %bitcast.4, f32[1,2048]{1,0:T(1,128)S(1)} %bitcast.5, s32[1,1]{1,0:T(1,128)S(6)} %copy.14.reach_ref, ...), custom_call_target="tpu_custom_call" | custom-call | tf_op jit(solution)/shard_map/pallas_call | solution.py:305
  32.6 0.7 %copy.11 = f32[128,224]{0,1:T(8,128)} copy(f32[128,224]{1,0:T(8,128)S(1)} %get-tuple-element.3) | data formatting | bytes 229376 | tf_op jit(solution)/shard_map/pallas_call | solution.py:305
  33.3 0.7 %copy.12 = f32[128,224]{0,1:T(8,128)} copy(f32[128,224]{1,0:T(8,128)S(1)} %get-tuple-element.4) | data formatting | bytes 229376 | tf_op jit(solution)/shard_map/pallas_call | solution.py:305
  34.1 0.7 %copy.13 = f32[128,224]{0,1:T(8,128)} copy(f32[128,224]{1,0:T(8,128)S(1)} %get-tuple-element.5) | data formatting | bytes 229376 | tf_op jit(solution)/shard_map/pallas_call | solution.py:305
Async XLA Ops:
  2.3 1.7 %copy-start = (f32[10,16,16,256]{3,2,1,0:T(8,128)S(1)}, f32[10,16,16,256]{3,2,1,0:T(8,128)}, u32[]{:S(2)}) copy-start(f32[10,16,16,256]{3,2,1,0:T(8,128)} %factors_ref.1) | copy-start | bytes 7864324
  4.0 0.8 %copy-start.1 = (f32[16,512]{1,0:T(8,128)S(1)}, f32[16,512]{1,0:T(8,128)}, u32[]{:S(2)}) copy-start(f32[16,512]{1,0:T(8,128)} %coarse_ref.1) | copy-start | bytes 98308
  4.8 0.7 %copy-start.2 = (s32[1,1,2048]{2,1,0:T(1,128)S(1)}, s32[1,1,2048]{2,1,0:T(1,128)}, u32[]{:S(2)}) copy-start(s32[1,1,2048]{2,1,0:T(1,128)} %param.8) | copy-start | bytes 24580
  5.5 0.7 %copy-start.3 = (f32[1,1,2048]{2,1,0:T(1,128)S(1)}, f32[1,1,2048]{2,1,0:T(1,128)}, u32[]{:S(2)}) copy-start(f32[1,1,2048]{2,1,0:T(1,128)} %param.9) | copy-start | bytes 24580
  6.2 0.7 %copy-start.4 = (f32[1,1,2048]{2,1,0:T(1,128)S(1)}, f32[1,1,2048]{2,1,0:T(1,128)}, u32[]{:S(2)}) copy-start(f32[1,1,2048]{2,1,0:T(1,128)} %param.10) | copy-start | bytes 24580

commit v2 on v1

v2 whole, which is shorter than its diff:
```python
import functools

import jax
import jax.numpy as jnp
from jax import lax
from jax.experimental import pallas as pl
from jax.experimental.pallas import tpu as pltpu
from jax.sharding import PartitionSpec as P

HW = 16
SUB = 4
DAMPING = 0.02
LANES = 128
F32 = jnp.float32
BF16 = jnp.bfloat16


def iota(shape, dim):
    return lax.broadcasted_iota(jnp.int32, shape, dim)


QUARTER = 2 * HW


def pack(x, start):
    groups = LANES // QUARTER
    size = x.shape[0] // groups
    at = iota((size, LANES), 1) // QUARTER
    whole = jnp.zeros((size, LANES), F32)
    for g in range(groups):
        part = x[g * size : (g + 1) * size]
        shift = (g * QUARTER - start) % LANES
        part = pltpu.roll(part, shift, 1) if shift else part
        whole = jnp.where(at == g, part, whole)
    return whole


def unpack(x, start):
    groups = LANES // QUARTER
    at = iota(x.shape, 1)
    parts = []
    for g in range(groups):
        shift = (start - g * QUARTER) % LANES
        part = pltpu.roll(x, shift, 1) if shift else x
        parts.append(jnp.where((at >= start) & (at < start + QUARTER), part, 0.0))
    return jnp.concatenate(parts, axis=0)


def kernel(
    n_lat, n_lon,
    sea_hbm, cell_hbm, value_hbm, weight_hbm, reach_ref, factors_hbm, coarse_hbm,
    sol_ref, res_ref, pre_ref,
    sea_ref, cell_ref, value_ref, weight_ref, fac, coarse_ref,
    diag, core, wide, edge, edge_in, corner, rows_in, corner_in, near, gather,
    contrib, side, side_in, band_in, cross, cross_in, total, mine, lat_in, half, lon_in,
    load_sem, send_sem, recv_sem,
):
    cx, cy = sea_ref.shape
    h, w = cy + 2 * HW, cx + 2 * HW
    i, j = lax.axis_index("lat"), lax.axis_index("lon")

    def lat_peer(o):
        return lax.rem(i + o + n_lat, n_lat)

    def lon_peer(o):
        return lax.rem(j + o + n_lon, n_lon)

    loads = [
        pltpu.make_async_copy(src, dst, load_sem.at[k])
        for k, (src, dst) in enumerate(
            (
                (cell_hbm, cell_ref),
                (weight_hbm, weight_ref),
                (value_hbm, value_ref),
                (sea_hbm, sea_ref),
                (coarse_hbm, coarse_ref),
                (factors_hbm, fac),
            )
        )
    ]
    for load in loads:
        load.start()

    barrier = pltpu.get_barrier_semaphore()

    def greet(pi, pj):
        pl.semaphore_signal(
            barrier, inc=1, device_id={"lat": pi, "lon": pj}, device_id_type=pl.DeviceIdType.MESH
        )

    corners = [(-1, -1), (-1, 1), (1, -1), (1, 1)]
    for o in range(1, n_lat):
        greet(lat_peer(o), j)
    for o in range(1, n_lon):
        greet(i, lon_peer(o))
    for di, dj in corners:
        greet(lat_peer(di), lon_peer(dj))

    used = [0]

    def remote(src, dst, pi, pj):
        k = used[0]
        used[0] += 1
        copy = pltpu.make_async_remote_copy(
            src_ref=src,
            dst_ref=dst,
            send_sem=send_sem.at[k],
            recv_sem=recv_sem.at[k],
            device_id={"lat": pi, "lon": pj},
            device_id_type=pl.DeviceIdType.MESH,
        )
        copy.start()
        return copy

    for load in loads[:4]:
        load.wait()
    blank = jnp.zeros((HW, cy), F32)
    ocean = jnp.concatenate([blank, sea_ref[...].astype(F32), blank], axis=0).T
    count = cell_ref.shape[2]
    chunk = 512 if count % 512 == 0 else count
    sums = jnp.zeros((4 * cy, w), F32)
    for at in range(0, count, chunk):
        cell = cell_ref[0, :, at : at + chunk].astype(F32)
        row = jnp.floor((cell + 0.5) * (1.0 / cx))
        col = cell - row * cx + HW
        weight = weight_ref[0, :, at : at + chunk]
        product = weight * value_ref[0, :, at : at + chunk]
        in_row = iota((cy, chunk), 0).astype(F32) == row
        in_col = iota((w, chunk), 0).astype(F32) == col
        parts = []
        for x in (weight, product):
            high = x.astype(BF16).astype(F32)
            parts += [high, x - high]
        left = jnp.concatenate([jnp.where(in_row, x, 0.0).astype(BF16) for x in parts], axis=0)
        right = jnp.where(in_col, 1.0, 0.0).astype(BF16)
        sums = sums + lax.dot_general(
            left, right, (((1,), (1,)), ((), ())), preferred_element_type=F32
        )
    diag[...] = sums[0:cy] + sums[cy : 2 * cy]
    rhs = ocean * (sums[2 * cy : 3 * cy] + sums[3 * cy : 4 * cy])
    core[0] = ocean
    core[1] = rhs

    block = cy // SUB
    lane_w = iota((SUB, w), 1) - HW
    sub_w = iota((SUB, w), 0) * (cx // SUB)
    group = jnp.where((lane_w >= sub_w) & (lane_w < sub_w + cx // SUB), 1.0, 0.0)
    strips = [
        jnp.sum(rhs[s * block : (s + 1) * block], axis=0, keepdims=True) * group for s in range(SUB)
    ]
    own = jnp.sum(jnp.concatenate(strips, axis=0), axis=1, keepdims=True)
    entries = SUB * SUB
    spot = iota((entries, LANES), 0) == (iota((entries, LANES), 1) % entries)
    own = jnp.sum(jnp.where(spot, own, 0.0), axis=0, keepdims=True)
    near[i] = own

    lane = iota((cy, LANES), 1)
    hi = w - LANES
    left = jnp.where(lane < QUARTER, ocean[:, :LANES], pltpu.roll(rhs[:, :LANES], HW, 1))
    right = jnp.where(lane >= LANES - HW, pltpu.roll(rhs[:, hi:], HW, 1), ocean[:, hi:])
    strips = (left, HW), (right, LANES - 2 * HW)
    for v, (x, start) in enumerate(strips):
        edge[v] = pack(x, start)
    for k, (di, dj) in enumerate(corners):
        x = strips[0 if dj < 0 else 1][0]
        corner[k] = x[0:HW] if di < 0 else x[cy - HW : cy]

    pl.semaphore_wait(barrier, n_lat - 1 + n_lon - 1 + 4)

    first = [remote(near.at[i], near.at[i], lat_peer(o), j) for o in range(1, n_lat)]
    halo = [
        remote(edge.at[0], edge_in.at[1], i, lon_peer(-1)),
        remote(edge.at[1], edge_in.at[0], i, lon_peer(1)),
        remote(core.at[:, pl.ds(0, HW)], rows_in.at[1], lat_peer(-1), j),
        remote(core.at[:, pl.ds(cy - HW, HW)], rows_in.at[0], lat_peer(1), j),
    ]
    for k, (di, dj) in enumerate(corners):
        halo.append(remote(corner.at[k], corner_in.at[3 - k], lat_peer(di), lon_peer(dj)))
    for copy in first:
        copy.wait()
    per = LANES // entries
    slot = iota((1, LANES), 1) // entries
    joint = min(n_lat, per)
    for q in range(n_lat // joint):
        line = jnp.zeros((1, LANES), F32)
        for r in range(joint):
            line = jnp.where(slot % joint == r, near[q * joint + r], line)
        gather[j, q] = line
    second = [remote(gather.at[j], gather.at[j], i, lon_peer(o)) for o in range(1, n_lon)]
    for copy in halo:
        copy.wait()

    def west(x):
        at = iota(x.shape, 1)
        return (
            jnp.where(at < HW, pltpu.roll(x, 2 * HW, 1), 0.0),
            jnp.where(at < HW, pltpu.roll(x, HW, 1), 0.0),
        )

    def east(x):
        at = iota(x.shape, 1)
        return (
            jnp.where(at >= LANES - HW, pltpu.roll(x, LANES - 2 * HW, 1), 0.0),
            jnp.where(at >= LANES - HW, pltpu.roll(x, LANES - 3 * HW, 1), 0.0),
        )

    spans = (
        (0, HW, rows_in.at[0], corner_in[0], corner_in[1], jnp.where(i > 0, 1.0, 0.0)),
        (HW, cy, core, unpack(edge_in[0], LANES - QUARTER), unpack(edge_in[1], HW), None),
        (HW + cy, HW, rows_in.at[1], corner_in[2], corner_in[3], jnp.where(i < n_lat - 1, 1.0, 0.0)),
    )
    for at, size, middle, left, right, inside in spans:
        for f, (lo, up) in enumerate(zip(west(left), east(right))):
            whole = middle[f]
            if inside is not None:
                whole, lo, up = whole * inside, lo * inside, up * inside
            wide[f, at : at + size, :] = whole
            wide[f, at : at + size, 0:LANES] += lo
            wide[f, at : at + size, hi:w] += up

    reach = reach_ref[0, 0]
    for load in loads[4:]:
        load.wait()
    col_pos = iota((HW, w), 1)
    col_ok = (col_pos >= HW - reach) & (col_pos < HW + cx + reach)
    blocks, size = fac.shape[0], fac.shape[1]
    for k in range(blocks):
        at = k * size
        row_pos = iota((size, w), 0) + at
        ok = col_ok & (row_pos >= HW - reach) & (row_pos < HW + cy + reach)
        scale = jnp.where(ok, wide[0, at : at + size], 0.0)
        u = scale * wide[1, at : at + size]
        g = jnp.zeros((size, w), F32)
        for p in range(size):
            row = fac[k, p]
            g = g + row * jnp.sum(row * u, axis=0, keepdims=True)
        contrib[at : at + size, :] = scale * g

    for copy in second:
        copy.wait()
    answer = jnp.zeros((entries, LANES), F32)
    for k in range(n_lat * n_lon // per):
        piece = jnp.zeros((1, LANES), F32)
        for r in range(0, per, joint):
            d = k * per + r
            piece = jnp.where(slot // joint == r // joint, gather[d // n_lat, d % n_lat // joint], piece)
        answer = answer + coarse_ref[:, k * LANES : (k + 1) * LANES] * piece
    answer = jnp.sum(answer, axis=1, keepdims=True)
    for s in range(SUB):
        line = jnp.sum(answer[s * SUB : (s + 1) * SUB] * group, axis=0, keepdims=True)
        at = HW + s * block
        contrib[at : at + block, :] += core[0, s * block : (s + 1) * block, :] * line

    deep = 2 * HW
    side[0] = pack(contrib[:, 0:LANES], 0)
    side[1] = pack(contrib[:, hi:w], LANES - deep)
    for k, (di, dj) in enumerate(corners):
        top = 0 if di < 0 else h - deep
        begin, start = (0, 0) if dj < 0 else (hi, LANES - deep)
        cross[k] = pack(contrib[top : top + deep, begin : begin + LANES], start)
    back = [
        remote(side.at[0], side_in.at[1], i, lon_peer(-1)),
        remote(side.at[1], side_in.at[0], i, lon_peer(1)),
        remote(contrib.at[pl.ds(0, deep)], band_in.at[1], lat_peer(-1), j),
        remote(contrib.at[pl.ds(h - deep, deep)], band_in.at[0], lat_peer(1), j),
    ]
    for k, (di, dj) in enumerate(corners):
        back.append(remote(cross.at[k], cross_in.at[3 - k], lat_peer(di), lon_peer(dj)))
    total[...] = contrib[...]
    for copy in back:
        copy.wait()

    total[:, 0:LANES] += unpack(side_in[0], 0)
    total[:, hi:w] += unpack(side_in[1], LANES - deep)
    for v in range(2):
        at = v * (h - deep)
        total[at : at + deep, :] += band_in[v]
        total[at : at + deep, 0:LANES] += unpack(cross_in[2 * v], 0)
        total[at : at + deep, hi:w] += unpack(cross_in[2 * v + 1], LANES - deep)

    p = total[HW : HW + cy, :]
    o = core[0]
    on, os = wide[0, HW - 1 : HW - 1 + cy, :], wide[0, HW + 1 : HW + 1 + cy, :]
    mid = wide[0, HW : HW + cy, :]
    oe, ow = pltpu.roll(mid, w - 1, 1), pltpu.roll(mid, 1, 1)
    beside = (
        oe * pltpu.roll(p, w - 1, 1)
        + ow * pltpu.roll(p, 1, 1)
        + on * total[HW - 1 : HW - 1 + cy, :]
        + os * total[HW + 1 : HW + 1 + cy, :]
    )
    image = o * ((diag[...] + DAMPING) * p + ((oe + ow + on + os) * p - beside)) + (1.0 - o) * p
    at = iota((cy, w), 1)
    inner = (at >= HW) & (at < HW + cx)

    def fold(x):
        x = jnp.sum(x, axis=0, keepdims=True)
        return sum(x[:, b : b + LANES] for b in range(0, w, LANES))

    mine[0:1] = fold(core[1] * p)
    mine[1:2] = fold(jnp.where(inner, p * image, 0.0))
    third = [remote(mine, lat_in.at[o - 1], lat_peer(o), j) for o in range(1, n_lat)]
    pre_ref[...] = p.T[HW : HW + cx]
    partial = mine[...]
    for o in range(1, n_lat):
        third[o - 1].wait()
        partial = partial + lat_in[o - 1]
    half[...] = partial
    fourth = [remote(half, lon_in.at[o - 1], i, lon_peer(o)) for o in range(1, n_lon)]
    rhs_out = core[1].T[HW : HW + cx]
    image_out = image.T[HW : HW + cx]
    for o in range(1, n_lon):
        fourth[o - 1].wait()
        partial = partial + lon_in[o - 1]
    rho = jnp.sum(partial[0:1], axis=1, keepdims=True)
    curve = jnp.sum(partial[1:2], axis=1, keepdims=True)
    alpha = rho / curve
    sol_ref[...] = alpha * pre_ref[...]
    res_ref[...] = rhs_out - alpha * image_out


def body(land_sea, obs_cell, obs_value, obs_weight, intersection, factors, coarse_inverse):
    n_lat, n_lon = lax.axis_size("lat"), lax.axis_size("lon")
    cy, cx = land_sea.shape
    h, w = cy + 2 * HW, cx + 2 * HW
    copies = 2 * (n_lat - 1 + n_lon - 1) + 16
    vmem = pl.BlockSpec(memory_space=pltpu.VMEM)
    entries = SUB * SUB
    lines = n_lat // min(n_lat, LANES // entries)
    hbm = pl.BlockSpec(memory_space=pltpu.HBM)
    out = jax.ShapeDtypeStruct((cx, cy), F32)
    results = pl.pallas_call(
        functools.partial(kernel, n_lat, n_lon),
        out_shape=(out, out, out),
        in_specs=[hbm, hbm, hbm, hbm, pl.BlockSpec(memory_space=pltpu.SMEM), hbm, hbm],
        out_specs=(vmem, vmem, vmem),
        scratch_shapes=[
            pltpu.VMEM((cx, cy), jnp.int32),
            pltpu.VMEM(obs_cell.shape, jnp.int32),
            pltpu.VMEM(obs_value.shape, F32),
            pltpu.VMEM(obs_weight.shape, F32),
            pltpu.VMEM(factors.shape, F32),
            pltpu.VMEM(coarse_inverse.shape, F32),
            pltpu.VMEM((cy, w), F32),
            pltpu.VMEM((2, cy, w), F32),
            pltpu.VMEM((2, h, w), F32),
            pltpu.VMEM((2, cy // 4, LANES), F32),
            pltpu.VMEM((2, cy // 4, LANES), F32),
            pltpu.VMEM((4, HW, LANES), F32),
            pltpu.VMEM((2, 2, HW, w), F32),
            pltpu.VMEM((4, HW, LANES), F32),
            pltpu.VMEM((n_lat, 1, LANES), F32),
            pltpu.VMEM((n_lon, lines, 1, LANES), F32),
            pltpu.VMEM((h, w), F32),
            pltpu.VMEM((2, h // 4, LANES), F32),
            pltpu.VMEM((2, h // 4, LANES), F32),
            pltpu.VMEM((2, 2 * HW, w), F32),
            pltpu.VMEM((4, HW // 2, LANES), F32),
            pltpu.VMEM((4, HW // 2, LANES), F32),
            pltpu.VMEM((h, w), F32),
            pltpu.VMEM((2, LANES), F32),
            pltpu.VMEM((n_lat - 1, 2, LANES), F32),
            pltpu.VMEM((2, LANES), F32),
            pltpu.VMEM((n_lon - 1, 2, LANES), F32),
            pltpu.SemaphoreType.DMA((6,)),
            pltpu.SemaphoreType.DMA((copies,)),
            pltpu.SemaphoreType.DMA((copies,)),
        ],
        compiler_params=pltpu.CompilerParams(
            collective_id=0, has_side_effects=True, vmem_limit_bytes=64 * 1024 * 1024
        ),
    )(land_sea.T, obs_cell, obs_value, obs_weight, intersection, factors, coarse_inverse)
    return tuple(x.T for x in results)


def solution(mesh):
    in_specs = (
        P("lat", "lon"),
        P("lat", "lon", None),
        P("lat", "lon", None),
        P("lat", "lon", None),
        P("lat", "lon"),
        P("lat", None, None, "lon"),
        P(("lon", "lat"), None),
    )
    out_specs = (P("lat", "lon"), P("lat", "lon"), P("lat", "lon"))
    return jax.shard_map(body, mesh=mesh, in_specs=in_specs, out_specs=out_specs, check_vma=False)
```

time: 35.2 us -> 30.7 us (0.87)
  local copies, waits for them, and re-layouts: 7.81 us -> 4.65 us
  Pallas kernels: 25.7 us -> 24.5 us
    pallas_call x3 -> x0, local copies, waits for them, and re-layouts: 2.24 us -> none  [body(): pl.pallas_call(functools.partial(kernel, n_lat, n_lon), out_shape=(out, o...]
    pallas_call x1, Pallas kernels: 25.7 us -> 24.5 us  [body(): pl.pallas_call(functools.partial(kernel, n_lat, n_lon), out_shape=(out, o...]
    unnamed x11 -> x3, local copies, waits for them, and re-layouts: 5.57 us -> 4.65 us
where the time goes in v2:
time: 30.7 us; the launch traced here: 30.4 us
  Pallas kernels  24.5 us (80%)
  local copies, waits for them, and re-layouts  4.65 us (15%)
  between operations  1.29 us (4%)
    pallas_call x1, Pallas kernels, body(): pl.pallas_call(functools.partial(kernel, n_lat, n_lon), out_shape=(out, o...  24.5 us
    unnamed x3, local copies, waits for them, and re-layouts  4.65 us

profile of v2, /device:TPU:0, one launch (start us, length us, event | category | flops | bytes accessed | tf_op | source)
XLA Modules:
  0.0 30.4 jit_solution(3178629332928722930)
XLA Ops:
  1.3 24.5 %shard_map.94 = (f32[224,128]{1,0:T(8,128)}, f32[224,128]{1,0:T(8,128)}, f32[224,128]{1,0:T(8,128)}) custom-call(s32[224,128]{1,0:T(8,128)} %bitcast.7, s32[1,1,2048]{2,1,0:T(1,128)} %cell_hbm.1, f32[1,1,2048]{2,1,0:T(1,128)} %value_hbm.1, f32[1,1,2048]{2,1,0:T(1,128)} %weight_hbm.1, s32[1,1]{1,0:T(1,128)S(6)} %copy.13.reach_ref, ...), custom_call_target="tpu_custom_call" | custom-call | tf_op jit(solution)/shard_map/pallas_call | solution.py:332
  25.8 1.6 %copy.14 = f32[128,224]{0,1:T(8,128)} copy(f32[128,224]{0,1:T(8,128)} %bitcast.6) | data formatting | bytes 229376
  27.3 1.6 %copy.15 = f32[128,224]{0,1:T(8,128)} copy(f32[128,224]{0,1:T(8,128)} %bitcast.5) | data formatting | bytes 229376
  28.9 1.6 %copy.16 = f32[128,224]{0,1:T(8,128)} copy(f32[128,224]{0,1:T(8,128)} %bitcast.4) | data formatting | bytes 229376

commit v3 on v2

--- a/solution.py
+++ b/solution.py
@@ -49,11 +49,11 @@
 def kernel(
     n_lat, n_lon,
     sea_hbm, cell_hbm, value_hbm, weight_hbm, reach_ref, factors_hbm, coarse_hbm,
-    sol_ref, res_ref, pre_ref,
+    pre_hbm, rhs_hbm, image_hbm, alpha_ref,
     sea_ref, cell_ref, value_ref, weight_ref, fac, coarse_ref,
     diag, core, wide, edge, edge_in, corner, rows_in, corner_in, near, gather,
-    contrib, side, side_in, band_in, cross, cross_in, total, mine, lat_in, half, lon_in,
-    load_sem, send_sem, recv_sem,
+    contrib, side, side_in, band_in, cross, cross_in, total, mine, lat_in, half, lon_in, out,
+    load_sem, store_sem, send_sem, recv_sem,
 ):
     cx, cy = sea_ref.shape
     h, w = cy + 2 * HW, cx + 2 * HW
@@ -300,23 +300,33 @@
     mine[0:1] = fold(core[1] * p)
     mine[1:2] = fold(jnp.where(inner, p * image, 0.0))
     third = [remote(mine, lat_in.at[o - 1], lat_peer(o), j) for o in range(1, n_lat)]
-    pre_ref[...] = p.T[HW : HW + cx]
+    stores = []
+    for k, (x, dst) in enumerate(((p, pre_hbm), (core[1], rhs_hbm), (image, image_hbm))):
+        out[k] = x.T[HW : HW + cx]
+        stores.append(pltpu.make_async_copy(out.at[k], dst, store_sem.at[k]))
+        stores[k].start()
     partial = mine[...]
     for o in range(1, n_lat):
         third[o - 1].wait()
         partial = partial + lat_in[o - 1]
     half[...] = partial
     fourth = [remote(half, lon_in.at[o - 1], i, lon_peer(o)) for o in range(1, n_lon)]
-    rhs_out = core[1].T[HW : HW + cx]
-    image_out = image.T[HW : HW + cx]
     for o in range(1, n_lon):
         fourth[o - 1].wait()
         partial = partial + lon_in[o - 1]
     rho = jnp.sum(partial[0:1], axis=1, keepdims=True)
     curve = jnp.sum(partial[1:2], axis=1, keepdims=True)
-    alpha = rho / curve
-    sol_ref[...] = alpha * pre_ref[...]
-    res_ref[...] = rhs_out - alpha * image_out
+    alpha_ref[...] = jnp.broadcast_to(rho / curve, alpha_ref.shape)
+    for store in stores:
+        store.wait()
+
+
+def finish(pre_ref, rhs_ref, image_ref, alpha_ref, sol_ref, res_ref, out_ref):
+    alpha = alpha_ref[0:1, 0:1]
+    pre = pre_ref[...]
+    out_ref[...] = pre
+    sol_ref[...] = alpha * pre
+    res_ref[...] = rhs_ref[...] - alpha * image_ref[...]
 
 
 def body(land_sea, obs_cell, obs_value, obs_weight, intersection, factors, coarse_inverse):
@@ -329,11 +339,11 @@
     lines = n_lat // min(n_lat, LANES // entries)
     hbm = pl.BlockSpec(memory_space=pltpu.HBM)
     out = jax.ShapeDtypeStruct((cx, cy), F32)
-    results = pl.pallas_call(
+    fields = pl.pallas_call(
         functools.partial(kernel, n_lat, n_lon),
-        out_shape=(out, out, out),
+        out_shape=(out, out, out, jax.ShapeDtypeStruct((8, LANES), F32)),
         in_specs=[hbm, hbm, hbm, hbm, pl.BlockSpec(memory_space=pltpu.SMEM), hbm, hbm],
-        out_specs=(vmem, vmem, vmem),
+        out_specs=(hbm, hbm, hbm, vmem),
         scratch_shapes=[
             pltpu.VMEM((cx, cy), jnp.int32),
             pltpu.VMEM(obs_cell.shape, jnp.int32),
@@ -362,7 +372,9 @@
             pltpu.VMEM((n_lat - 1, 2, LANES), F32),
             pltpu.VMEM((2, LANES), F32),
             pltpu.VMEM((n_lon - 1, 2, LANES), F32),
+            pltpu.VMEM((3, cx, cy), F32),
             pltpu.SemaphoreType.DMA((6,)),
+            pltpu.SemaphoreType.DMA((3,)),
             pltpu.SemaphoreType.DMA((copies,)),
             pltpu.SemaphoreType.DMA((copies,)),
         ],
@@ -370,6 +382,13 @@
             collective_id=0, has_side_effects=True, vmem_limit_bytes=64 * 1024 * 1024
         ),
     )(land_sea.T, obs_cell, obs_value, obs_weight, intersection, factors, coarse_inverse)
+    results = pl.pallas_call(
+        finish,
+        out_shape=(out, out, out),
+        in_specs=[vmem] * 4,
+        out_specs=(vmem, vmem, vmem),
+        compiler_params=pltpu.CompilerParams(vmem_limit_bytes=64 * 1024 * 1024),
+    )(*fields)
     return tuple(x.T for x in results)
 
 

time: 30.7 us -> 27.7 us (0.902)
  local copies, waits for them, and re-layouts: 4.65 us -> 0 us
  Pallas kernels: 24.5 us -> 26.2 us
    unnamed x3 -> x0, local copies, waits for them, and re-layouts: 4.65 us -> none
    pallas_call x0 -> x1, Pallas kernels: none -> 1.78 us  [body(): pl.pallas_call(finish, out_shape=(out, out, out), in_specs=[vmem] * 4, ou...]
where the time goes in v3:
time: 27.7 us; the launch traced here: 27.5 us
  Pallas kernels  26.2 us (95%)
  between operations  1.29 us (5%)
    pallas_call x1, Pallas kernels, body(): pl.pallas_call(functools.partial(kernel, n_lat, n_lon), out_shape=(out, o...  24.4 us
    pallas_call x1, Pallas kernels, body(): pl.pallas_call(finish, out_shape=(out, out, out), in_specs=[vmem] * 4, ou...  1.78 us

profile of v3, /device:TPU:0, one launch (start us, length us, event | category | flops | bytes accessed | tf_op | source)
XLA Modules:
  0.0 27.5 jit_solution(3487358715719151476)
XLA Ops:
  1.3 24.4 %shard_map.94 = (f32[224,128]{1,0:T(8,128)}, f32[224,128]{1,0:T(8,128)}, f32[224,128]{1,0:T(8,128)}, f32[8,128]{1,0:T(8,128)}) custom-call(s32[224,128]{1,0:T(8,128)} %bitcast.4, s32[1,1,2048]{2,1,0:T(1,128)} %cell_hbm.1, f32[1,1,2048]{2,1,0:T(1,128)} %value_hbm.1, f32[1,1,2048]{2,1,0:T(1,128)} %weight_hbm.1, s32[1,1]{1,0:T(1,128)S(6)} %copy.10.reach_ref, ...), custom_call_target="tpu_custom_call" | custom-call | tf_op jit(solution)/shard_map/pallas_call | solution.py:342
  25.7 1.8 %shard_map.95 = (f32[224,128]{1,0:T(8,128)}, f32[224,128]{1,0:T(8,128)}, f32[224,128]{1,0:T(8,128)}) custom-call(f32[224,128]{1,0:T(8,128)} %get-tuple-element.10.pre_ref, f32[224,128]{1,0:T(8,128)} %get-tuple-element.11.rhs_ref, f32[224,128]{1,0:T(8,128)} %get-tuple-element.12.image_ref, f32[8,128]{1,0:T(8,128)} %get-tuple-element.13.alpha_ref), custom_call_target="tpu_custom_call" | custom-call | tf_op jit(solution)/shard_map/pallas_call | solution.py:385

commit v4 on v3

--- a/solution.py
+++ b/solution.py
@@ -96,11 +96,10 @@
     for di, dj in corners:
         greet(lat_peer(di), lon_peer(dj))
 
-    used = [0]
+    sent = []
 
     def remote(src, dst, pi, pj):
-        k = used[0]
-        used[0] += 1
+        k = len(sent)
         copy = pltpu.make_async_remote_copy(
             src_ref=src,
             dst_ref=dst,
@@ -110,6 +109,7 @@
             device_id_type=pl.DeviceIdType.MESH,
         )
         copy.start()
+        sent.append(copy)
         return copy
 
     for load in loads[:4]:
@@ -118,6 +118,8 @@
     ocean = jnp.concatenate([blank, sea_ref[...].astype(F32), blank], axis=0).T
     count = cell_ref.shape[2]
     chunk = 512 if count % 512 == 0 else count
+    spot_type = BF16 if max(cy, w) <= 256 else F32
+    none, one = jnp.zeros((), BF16), jnp.ones((), BF16)
     sums = jnp.zeros((4 * cy, w), F32)
     for at in range(0, count, chunk):
         cell = cell_ref[0, :, at : at + chunk].astype(F32)
@@ -125,14 +127,14 @@
         col = cell - row * cx + HW
         weight = weight_ref[0, :, at : at + chunk]
         product = weight * value_ref[0, :, at : at + chunk]
-        in_row = iota((cy, chunk), 0).astype(F32) == row
-        in_col = iota((w, chunk), 0).astype(F32) == col
+        in_row = iota((cy, chunk), 0).astype(F32).astype(spot_type) == row.astype(spot_type)
+        in_col = iota((w, chunk), 0).astype(F32).astype(spot_type) == col.astype(spot_type)
         parts = []
         for x in (weight, product):
-            high = x.astype(BF16).astype(F32)
-            parts += [high, x - high]
-        left = jnp.concatenate([jnp.where(in_row, x, 0.0).astype(BF16) for x in parts], axis=0)
-        right = jnp.where(in_col, 1.0, 0.0).astype(BF16)
+            high = x.astype(BF16)
+            parts += [high, (x - high.astype(F32)).astype(BF16)]
+        left = jnp.concatenate([jnp.where(in_row, x, none) for x in parts], axis=0)
+        right = jnp.where(in_col, one, none)
         sums = sums + lax.dot_general(
             left, right, (((1,), (1,)), ((), ())), preferred_element_type=F32
         )
@@ -177,7 +179,7 @@
     for k, (di, dj) in enumerate(corners):
         halo.append(remote(corner.at[k], corner_in.at[3 - k], lat_peer(di), lon_peer(dj)))
     for copy in first:
-        copy.wait()
+        copy.wait_recv()
     per = LANES // entries
     slot = iota((1, LANES), 1) // entries
     joint = min(n_lat, per)
@@ -188,7 +190,7 @@
         gather[j, q] = line
     second = [remote(gather.at[j], gather.at[j], i, lon_peer(o)) for o in range(1, n_lon)]
     for copy in halo:
-        copy.wait()
+        copy.wait_recv()
 
     def west(x):
         at = iota(x.shape, 1)
@@ -237,7 +239,7 @@
         contrib[at : at + size, :] = scale * g
 
     for copy in second:
-        copy.wait()
+        copy.wait_recv()
     answer = jnp.zeros((entries, LANES), F32)
     for k in range(n_lat * n_lon // per):
         piece = jnp.zeros((1, LANES), F32)
@@ -268,7 +270,7 @@
         back.append(remote(cross.at[k], cross_in.at[3 - k], lat_peer(di), lon_peer(dj)))
     total[...] = contrib[...]
     for copy in back:
-        copy.wait()
+        copy.wait_recv()
 
     total[:, 0:LANES] += unpack(side_in[0], 0)
     total[:, hi:w] += unpack(side_in[1], LANES - deep)
@@ -307,16 +309,18 @@
         stores[k].start()
     partial = mine[...]
     for o in range(1, n_lat):
-        third[o - 1].wait()
+        third[o - 1].wait_recv()
         partial = partial + lat_in[o - 1]
     half[...] = partial
     fourth = [remote(half, lon_in.at[o - 1], i, lon_peer(o)) for o in range(1, n_lon)]
     for o in range(1, n_lon):
-        fourth[o - 1].wait()
+        fourth[o - 1].wait_recv()
         partial = partial + lon_in[o - 1]
     rho = jnp.sum(partial[0:1], axis=1, keepdims=True)
     curve = jnp.sum(partial[1:2], axis=1, keepdims=True)
     alpha_ref[...] = jnp.broadcast_to(rho / curve, alpha_ref.shape)
+    for copy in sent:
+        copy.wait_send()
     for store in stores:
         store.wait()
 

time: 27.7 us -> 27.7 us (level)
  no operation moved by 1% of the time
where the time goes in v4:
time: 27.7 us; the launch traced here: 27.5 us
  Pallas kernels  26.2 us (95%)
  between operations  1.29 us (5%)
    pallas_call x1, Pallas kernels, body(): pl.pallas_call(functools.partial(kernel, n_lat, n_lon), out_shape=(out, o...  24.4 us
    pallas_call x1, Pallas kernels, body(): pl.pallas_call(finish, out_shape=(out, out, out), in_specs=[vmem] * 4, ou...  1.78 us

profile of v4, /device:TPU:0, one launch (start us, length us, event | category | flops | bytes accessed | tf_op | source)
XLA Modules:
  0.0 27.5 jit_solution(14137008788551725276)
XLA Ops:
  1.3 24.4 %shard_map.94 = (f32[224,128]{1,0:T(8,128)}, f32[224,128]{1,0:T(8,128)}, f32[224,128]{1,0:T(8,128)}, f32[8,128]{1,0:T(8,128)}) custom-call(s32[224,128]{1,0:T(8,128)} %bitcast.4, s32[1,1,2048]{2,1,0:T(1,128)} %cell_hbm.1, f32[1,1,2048]{2,1,0:T(1,128)} %value_hbm.1, f32[1,1,2048]{2,1,0:T(1,128)} %weight_hbm.1, s32[1,1]{1,0:T(1,128)S(6)} %copy.10.reach_ref, ...), custom_call_target="tpu_custom_call" | custom-call | tf_op jit(solution)/shard_map/pallas_call | solution.py:346
  25.7 1.8 %shard_map.95 = (f32[224,128]{1,0:T(8,128)}, f32[224,128]{1,0:T(8,128)}, f32[224,128]{1,0:T(8,128)}) custom-call(f32[224,128]{1,0:T(8,128)} %get-tuple-element.10.pre_ref, f32[224,128]{1,0:T(8,128)} %get-tuple-element.11.rhs_ref, f32[224,128]{1,0:T(8,128)} %get-tuple-element.12.image_ref, f32[8,128]{1,0:T(8,128)} %get-tuple-element.13.alpha_ref), custom_call_target="tpu_custom_call" | custom-call | tf_op jit(solution)/shard_map/pallas_call | solution.py:389

commit v5 on v3

--- a/solution.py
+++ b/solution.py
@@ -10,6 +10,7 @@
 HW = 16
 SUB = 4
 DAMPING = 0.02
+DIRECT = 64
 LANES = 128
 F32 = jnp.float32
 BF16 = jnp.bfloat16
@@ -89,12 +90,18 @@
         )
 
     corners = [(-1, -1), (-1, 1), (1, -1), (1, 1)]
-    for o in range(1, n_lat):
-        greet(lat_peer(o), j)
-    for o in range(1, n_lon):
-        greet(i, lon_peer(o))
-    for di, dj in corners:
-        greet(lat_peer(di), lon_peer(dj))
+    others = [(a, b) for a in range(n_lat) for b in range(n_lon) if a or b]
+    direct = len(others) < DIRECT
+    if direct:
+        for a, b in others:
+            greet(lat_peer(a), lon_peer(b))
+    else:
+        for o in range(1, n_lat):
+            greet(lat_peer(o), j)
+        for o in range(1, n_lon):
+            greet(i, lon_peer(o))
+        for di, dj in corners:
+            greet(lat_peer(di), lon_peer(dj))
 
     used = [0]
 
@@ -165,7 +172,7 @@
         x = strips[0 if dj < 0 else 1][0]
         corner[k] = x[0:HW] if di < 0 else x[cy - HW : cy]
 
-    pl.semaphore_wait(barrier, n_lat - 1 + n_lon - 1 + 4)
+    pl.semaphore_wait(barrier, len(others) if direct else n_lat - 1 + n_lon - 1 + 4)
 
     first = [remote(near.at[i], near.at[i], lat_peer(o), j) for o in range(1, n_lat)]
     halo = [
@@ -299,24 +306,37 @@
 
     mine[0:1] = fold(core[1] * p)
     mine[1:2] = fold(jnp.where(inner, p * image, 0.0))
-    third = [remote(mine, lat_in.at[o - 1], lat_peer(o), j) for o in range(1, n_lat)]
+    if direct:
+        third = [
+            remote(mine, lon_in.at[k], lat_peer(a), lon_peer(b)) for k, (a, b) in enumerate(others)
+        ]
+    else:
+        third = [remote(mine, lat_in.at[o - 1], lat_peer(o), j) for o in range(1, n_lat)]
     stores = []
     for k, (x, dst) in enumerate(((p, pre_hbm), (core[1], rhs_hbm), (image, image_hbm))):
         out[k] = x.T[HW : HW + cx]
         stores.append(pltpu.make_async_copy(out.at[k], dst, store_sem.at[k]))
         stores[k].start()
     partial = mine[...]
-    for o in range(1, n_lat):
-        third[o - 1].wait()
-        partial = partial + lat_in[o - 1]
-    half[...] = partial
-    fourth = [remote(half, lon_in.at[o - 1], i, lon_peer(o)) for o in range(1, n_lon)]
-    for o in range(1, n_lon):
-        fourth[o - 1].wait()
-        partial = partial + lon_in[o - 1]
+    if direct:
+        for k, copy in enumerate(third):
+            copy.wait_recv()
+            partial = partial + lon_in[k]
+    else:
+        for k, copy in enumerate(third):
+            copy.wait_recv()
+            partial = partial + lat_in[k]
+        half[...] = partial
+        fourth = [remote(half, lon_in.at[o - 1], i, lon_peer(o)) for o in range(1, n_lon)]
+        for k, copy in enumerate(fourth):
+            copy.wait_recv()
+            partial = partial + lon_in[k]
+        third = third + fourth
     rho = jnp.sum(partial[0:1], axis=1, keepdims=True)
     curve = jnp.sum(partial[1:2], axis=1, keepdims=True)
     alpha_ref[...] = jnp.broadcast_to(rho / curve, alpha_ref.shape)
+    for copy in third:
+        copy.wait_send()
     for store in stores:
         store.wait()
 
@@ -333,7 +353,9 @@
     n_lat, n_lon = lax.axis_size("lat"), lax.axis_size("lon")
     cy, cx = land_sea.shape
     h, w = cy + 2 * HW, cx + 2 * HW
-    copies = 2 * (n_lat - 1 + n_lon - 1) + 16
+    others = n_lat * n_lon - 1
+    sums = others if others < DIRECT else n_lon - 1
+    copies = 2 * (n_lat - 1) + n_lon - 1 + sums + 16
     vmem = pl.BlockSpec(memory_space=pltpu.VMEM)
     entries = SUB * SUB
     lines = n_lat // min(n_lat, LANES // entries)
@@ -371,7 +393,7 @@
             pltpu.VMEM((2, LANES), F32),
             pltpu.VMEM((n_lat - 1, 2, LANES), F32),
             pltpu.VMEM((2, LANES), F32),
-            pltpu.VMEM((n_lon - 1, 2, LANES), F32),
+            pltpu.VMEM((sums, 2, LANES), F32),
             pltpu.VMEM((3, cx, cy), F32),
             pltpu.SemaphoreType.DMA((6,)),
             pltpu.SemaphoreType.DMA((3,)),

time: 27.7 us -> 26.8 us (0.968)
  Pallas kernels: 26.2 us -> 25.3 us
    pallas_call x1, Pallas kernels: 24.4 us -> 23.5 us  [body(): pl.pallas_call(functools.partial(kernel, n_lat, n_lon), out_shape=(out, o...]
where the time goes in v5:
time: 26.8 us; the launch traced here: 26.6 us
  Pallas kernels  25.3 us (94%)
  between operations  1.29 us (5%)
    pallas_call x1, Pallas kernels, body(): pl.pallas_call(functools.partial(kernel, n_lat, n_lon), out_shape=(out, o...  23.5 us
    pallas_call x1, Pallas kernels, body(): pl.pallas_call(finish, out_shape=(out, out, out), in_specs=[vmem] * 4, ou...  1.78 us

profile of v5, /device:TPU:0, one launch (start us, length us, event | category | flops | bytes accessed | tf_op | source)
XLA Modules:
  0.0 26.6 jit_solution(13699019958830107207)
XLA Ops:
  1.3 23.5 %shard_map.94 = (f32[224,128]{1,0:T(8,128)}, f32[224,128]{1,0:T(8,128)}, f32[224,128]{1,0:T(8,128)}, f32[8,128]{1,0:T(8,128)}) custom-call(s32[224,128]{1,0:T(8,128)} %bitcast.4, s32[1,1,2048]{2,1,0:T(1,128)} %cell_hbm.1, f32[1,1,2048]{2,1,0:T(1,128)} %value_hbm.1, f32[1,1,2048]{2,1,0:T(1,128)} %weight_hbm.1, s32[1,1]{1,0:T(1,128)S(6)} %copy.10.reach_ref, ...), custom_call_target="tpu_custom_call" | custom-call | tf_op jit(solution)/shard_map/pallas_call | solution.py:364
  24.8 1.8 %shard_map.95 = (f32[224,128]{1,0:T(8,128)}, f32[224,128]{1,0:T(8,128)}, f32[224,128]{1,0:T(8,128)}) custom-call(f32[224,128]{1,0:T(8,128)} %get-tuple-element.10.pre_ref, f32[224,128]{1,0:T(8,128)} %get-tuple-element.11.rhs_ref, f32[224,128]{1,0:T(8,128)} %get-tuple-element.12.image_ref, f32[8,128]{1,0:T(8,128)} %get-tuple-element.13.alpha_ref), custom_call_target="tpu_custom_call" | custom-call | tf_op jit(solution)/shard_map/pallas_call | solution.py:407

commit v6 on v5

--- a/solution.py
+++ b/solution.py
@@ -124,7 +124,7 @@
     blank = jnp.zeros((HW, cy), F32)
     ocean = jnp.concatenate([blank, sea_ref[...].astype(F32), blank], axis=0).T
     count = cell_ref.shape[2]
-    chunk = 512 if count % 512 == 0 else count
+    chunk = 1024 if count % 1024 == 0 else count
     sums = jnp.zeros((4 * cy, w), F32)
     for at in range(0, count, chunk):
         cell = cell_ref[0, :, at : at + chunk].astype(F32)

time: 26.8 us -> 26.8 us (level)
  no operation moved by 1% of the time
where the time goes in v6:
time: 26.8 us; the launch traced here: 26.6 us
  Pallas kernels  25.3 us (94%)
  between operations  1.29 us (5%)
    pallas_call x1, Pallas kernels, body(): pl.pallas_call(functools.partial(kernel, n_lat, n_lon), out_shape=(out, o...  23.5 us
    pallas_call x1, Pallas kernels, body(): pl.pallas_call(finish, out_shape=(out, out, out), in_specs=[vmem] * 4, ou...  1.78 us

profile of v6, /device:TPU:0, one launch (start us, length us, event | category | flops | bytes accessed | tf_op | source)
XLA Modules:
  0.0 26.6 jit_solution(11992145021914652773)
XLA Ops:
  1.3 23.5 %shard_map.94 = (f32[224,128]{1,0:T(8,128)}, f32[224,128]{1,0:T(8,128)}, f32[224,128]{1,0:T(8,128)}, f32[8,128]{1,0:T(8,128)}) custom-call(s32[224,128]{1,0:T(8,128)} %bitcast.4, s32[1,1,2048]{2,1,0:T(1,128)} %cell_hbm.1, f32[1,1,2048]{2,1,0:T(1,128)} %value_hbm.1, f32[1,1,2048]{2,1,0:T(1,128)} %weight_hbm.1, s32[1,1]{1,0:T(1,128)S(6)} %copy.10.reach_ref, ...), custom_call_target="tpu_custom_call" | custom-call | tf_op jit(solution)/shard_map/pallas_call | solution.py:364
  24.8 1.8 %shard_map.95 = (f32[224,128]{1,0:T(8,128)}, f32[224,128]{1,0:T(8,128)}, f32[224,128]{1,0:T(8,128)}) custom-call(f32[224,128]{1,0:T(8,128)} %get-tuple-element.10.pre_ref, f32[224,128]{1,0:T(8,128)} %get-tuple-element.11.rhs_ref, f32[224,128]{1,0:T(8,128)} %get-tuple-element.12.image_ref, f32[8,128]{1,0:T(8,128)} %get-tuple-element.13.alpha_ref), custom_call_target="tpu_custom_call" | custom-call | tf_op jit(solution)/shard_map/pallas_call | solution.py:407
